TPU v7x, 32 devices: a whole 2x2x4 slice. The times are simulated.
32 devices in a mesh: batch: 8 (over y, x, core), seq: 4 (over z).
Axes of the slice: x: 2, y: 2, z: 4, core: 2. Of those that a mesh axis runs over, the one named last changes fastest.
Arguments:
- inputs: bfloat16 [32, 2048, 768], P('batch', 'seq'), may hold values from -6 to 6
- cotangent: bfloat16 [32, 2048, 768], P('batch', 'seq'), may hold values from -12 to 12
- set_kind: int32 [32], P('batch'), may hold values from 0 to 1, as said below
- row_offset: int32 [32, 4], P('batch'), may hold values from 0 to 1536, as said below
- query_w: bfloat16 [768, 768], replicated, may hold values from -0.21875 to 0.21875
- key_w: bfloat16 [768, 768], replicated, may hold values from -0.21875 to 0.21875
- value_w: bfloat16 [768, 768], replicated, may hold values from -0.21875 to 0.21875
- output_w: bfloat16 [768, 768], replicated, may hold values from -0.875 to 0.875
- up_w: bfloat16 [768, 3072], replicated, may hold values from -0.21875 to 0.21875
- down_w: bfloat16 [3072, 768], replicated, may hold values from -0.109375 to 0.109375
- compress: bfloat16 [2048, 256], replicated, may hold values from -0.1875 to 0.1875
- first_gain: float32 [768], replicated, may hold values from 0.1 to 1.9
- first_bias: float32 [768], replicated, may hold values from -3 to 3
- second_gain: float32 [768], replicated, may hold values from 0.1 to 1.9
- second_bias: float32 [768], replicated, may hold values from -3 to 3
Outputs:
- layer_out: bfloat16 [32, 2048, 768], P('batch', 'seq')
- input_grad: float32 [32, 2048, 768], P('batch', 'seq')
- query_grad: float32 [768, 768], P('batch', 'seq')
- key_grad: float32 [768, 768], P('batch', 'seq')
- value_grad: float32 [768, 768], P('batch', 'seq')
- output_grad: float32 [768, 768], P('batch', 'seq')
- up_grad: float32 [768, 3072], P('batch', 'seq')
- down_grad: float32 [3072, 768], P('batch', 'seq')
- compress_grad: float32 [2048, 256], replicated
- first_gain_grad: float32 [768], replicated
- first_bias_grad: float32 [768], replicated
- second_gain_grad: float32 [768], replicated
- second_bias_grad: float32 [768], replicated
Inputs may be any that keep to these rules, and one draw needn't show every extreme that they name: `set_kind`: the 4 consecutive sets of each batch index include at least one set that is a single sequence. `row_offset`: entries of a set that is a single sequence are not read.
All inputs are finite; a program needn't handle non-finite values.
Results may differ from a plain program's by a relative error of at most 0.028.
Values may be sent and summed in bfloat16 or wider, within the bound.
A program may use at most 256 MiB of HBM per device.

v0:
```python
import jax
import jax.numpy as jnp
from jax import lax
from jax.sharding import PartitionSpec as P

H = 12
DH = 64


def shifted(block, axis, distance):
    devices = range(lax.axis_size(axis))
    route = [((i - distance) % len(devices), i) for i in devices]
    return lax.ppermute(block, axis, route)


def layer_norm(values_in, gain_in, bias_in):
    average = jnp.mean(values_in, axis=-1, keepdims=True)
    centered = values_in - average
    variance = jnp.mean(centered * centered, axis=-1, keepdims=True)
    return centered * lax.rsqrt(variance + 1e-05) * gain_in + bias_in


def gelu_exact(values_in):
    return jax.nn.gelu(values_in, approximate=False)


def contract_rows(left_in, right_in):
    return lax.dot_general(
        left_in, right_in, (((0,), (0,)), ((), ())), preferred_element_type=jnp.float32
    )


def contract_cols(left_in, right_in):
    return lax.dot_general(
        left_in, right_in, (((1,), (1,)), ((), ())), preferred_element_type=jnp.float32
    )


def table_start(set_kind, row_offset, block_index, row_count, shortest):
    position = block_index * row_count
    member = position // shortest
    chosen = jnp.sum(jnp.where(jnp.arange(4)[None, :] == member, row_offset, 0), axis=1)
    return jnp.where(set_kind > 0, position, chosen + position % shortest)


def table_rows(compress, starts, row_count):

    def one_slice(row_begin):
        return lax.dynamic_slice_in_dim(compress, row_begin, row_count, 0)

    return jax.vmap(one_slice)(starts)


def local(
    inputs,
    cotangent,
    set_kind,
    row_offset,
    query_w,
    key_w,
    value_w,
    output_w,
    up_w,
    down_w,
    compress,
    first_gain,
    first_bias,
    second_gain,
    second_bias,
):
    set_count, row_count, model_width = inputs.shape
    longest, summary_rows = compress.shape
    shortest = longest // 4
    seq_count = lax.axis_size("seq")
    ranked = lax.axis_index("seq")
    token_count = set_count * row_count
    scale = DH ** (-0.5)
    is_long = set_kind > 0
    own_member = ranked * row_count // shortest
    own_start = table_start(set_kind, row_offset, ranked, row_count, shortest)
    own_table = table_rows(compress, own_start, row_count)
    flat_in = inputs.reshape(token_count, model_width)
    joined_w = jnp.concatenate([query_w, key_w, value_w], axis=1)
    projected = jnp.dot(flat_in, joined_w, preferred_element_type=jnp.float32).astype(jnp.bfloat16)
    queries = projected[:, :model_width].reshape(set_count, row_count, H, DH)
    packed = projected[:, model_width:].reshape(set_count, row_count, 2 * model_width)
    travel_init = jnp.einsum(
        "srk,srd->skd", own_table, packed, preferred_element_type=jnp.float32
    ).astype(jnp.bfloat16)

    def cycle_step(step_index, loop_state):
        travel, running = loop_state
        travel = shifted(travel, "seq", 1)
        source = (ranked - step_index) % seq_count
        joined = is_long | (source * row_count // shortest == own_member)
        return (travel, running + jnp.where(joined[:, None, None], travel.astype(jnp.float32), 0.0))

    final_travel, summary = lax.fori_loop(
        1, seq_count, cycle_step, (travel_init, travel_init.astype(jnp.float32))
    )
    summary_low = summary.astype(jnp.bfloat16)
    keys_c = summary_low[:, :, :model_width].reshape(set_count, summary_rows, H, DH)
    values_c = summary_low[:, :, model_width:].reshape(set_count, summary_rows, H, DH)
    scores = (
        jnp.einsum("srhd,skhd->shrk", queries, keys_c, preferred_element_type=jnp.float32) * scale
    )
    highest_score = jnp.max(scores, axis=-1, keepdims=True)
    log_total = highest_score + jnp.log(
        jnp.sum(jnp.exp(scores - highest_score), axis=-1, keepdims=True)
    )
    probs = jnp.exp(scores - log_total)
    probs_low = probs.astype(jnp.bfloat16)
    mixed = jnp.einsum("shrk,skhd->srhd", probs_low, values_c, preferred_element_type=jnp.float32)
    mixed_low = mixed.reshape(token_count, model_width).astype(jnp.bfloat16)
    attended = jnp.dot(mixed_low, output_w, preferred_element_type=jnp.float32)
    first_sum = flat_in.astype(jnp.float32) + attended
    hidden, first_back = jax.vjp(layer_norm, first_sum, first_gain, first_bias)
    hidden_low = hidden.astype(jnp.bfloat16)
    upward = jnp.dot(hidden_low, up_w, preferred_element_type=jnp.float32)
    activated, gelu_back = jax.vjp(gelu_exact, upward)
    activated_low = activated.astype(jnp.bfloat16)
    downward = jnp.dot(activated_low, down_w, preferred_element_type=jnp.float32)
    result, second_back = jax.vjp(layer_norm, hidden + downward, second_gain, second_bias)
    layer_out = result.astype(jnp.bfloat16).reshape(set_count, row_count, model_width)
    grad_second, second_gain_part, second_bias_part = second_back(
        cotangent.reshape(token_count, model_width).astype(jnp.float32)
    )
    grad_down = grad_second.astype(jnp.bfloat16)
    down_part = contract_rows(activated_low, grad_down)
    (grad_upward,) = gelu_back(contract_cols(grad_down, down_w))
    grad_up = grad_upward.astype(jnp.bfloat16)
    up_part = contract_rows(hidden_low, grad_up)
    grad_hidden = grad_second + contract_cols(grad_up, up_w)
    grad_first, first_gain_part, first_bias_part = first_back(grad_hidden)
    grad_attended = grad_first.astype(jnp.bfloat16)
    output_part = contract_rows(mixed_low, grad_attended)
    grad_mixed = (
        contract_cols(grad_attended, output_w)
        .astype(jnp.bfloat16)
        .reshape(set_count, row_count, H, DH)
    )
    grad_probs = jnp.einsum(
        "srhd,skhd->shrk", grad_mixed, values_c, preferred_element_type=jnp.float32
    )
    row_delta = jnp.sum(grad_probs * probs, axis=-1, keepdims=True)
    grad_scores = (probs * (grad_probs - row_delta)).astype(jnp.bfloat16)
    grad_queries = (
        jnp.einsum("shrk,skhd->srhd", grad_scores, keys_c, preferred_element_type=jnp.float32)
        * scale
    ).astype(jnp.bfloat16)
    grad_keys_c = (
        jnp.einsum("shrk,srhd->skhd", grad_scores, queries, preferred_element_type=jnp.float32)
        * scale
    )
    grad_values_c = jnp.einsum(
        "shrk,srhd->skhd", probs_low, grad_mixed, preferred_element_type=jnp.float32
    )
    grad_part = jnp.concatenate(
        [
            grad_keys_c.reshape(set_count, summary_rows, model_width),
            grad_values_c.reshape(set_count, summary_rows, model_width),
        ],
        axis=2,
    )

    def cycle_back(step_index, loop_state):
        travel, running = loop_state
        travel = shifted(travel.astype(jnp.bfloat16), "seq", -1).astype(travel.dtype)
        source = (ranked + step_index) % seq_count
        joined = is_long | (source * row_count // shortest == own_member)
        return (travel, running + jnp.where(joined[:, None, None], travel, 0.0))

    final_travel, grad_summary = lax.fori_loop(1, seq_count, cycle_back, (grad_part, grad_part))
    grad_summary_low = grad_summary.astype(jnp.bfloat16)
    grad_packed = jnp.einsum(
        "srk,skd->srd", own_table, grad_summary_low, preferred_element_type=jnp.float32
    ).astype(jnp.bfloat16)
    table_terms = jnp.einsum(
        "srd,skd->srk", packed, grad_summary_low, preferred_element_type=jnp.float32
    )
    compress_part = jnp.zeros((longest, summary_rows), jnp.float32)
    for set_index in range(set_count):
        current = lax.dynamic_slice_in_dim(compress_part, own_start[set_index], row_count, 0)
        compress_part = lax.dynamic_update_slice_in_dim(
            compress_part, current + table_terms[set_index], own_start[set_index], 0
        )
    grad_joined = jnp.concatenate(
        [
            grad_queries.reshape(token_count, model_width),
            grad_packed.reshape(token_count, 2 * model_width),
        ],
        axis=1,
    )
    joined_part = contract_rows(flat_in, grad_joined)
    input_grad = grad_first + contract_cols(grad_joined, joined_w)
    query_part = joined_part[:, :model_width]
    key_part = joined_part[:, model_width : 2 * model_width]
    value_part = joined_part[:, 2 * model_width :]
    seq_summed = (
        lax.psum_scatter(
            query_part.astype(jnp.bfloat16), "seq", scatter_dimension=1, tiled=True
        ).astype(jnp.float32),
        lax.psum_scatter(
            key_part.astype(jnp.bfloat16), "seq", scatter_dimension=1, tiled=True
        ).astype(jnp.float32),
        lax.psum_scatter(
            value_part.astype(jnp.bfloat16), "seq", scatter_dimension=1, tiled=True
        ).astype(jnp.float32),
        lax.psum_scatter(
            output_part.astype(jnp.bfloat16), "seq", scatter_dimension=1, tiled=True
        ).astype(jnp.float32),
        lax.psum_scatter(
            up_part.astype(jnp.bfloat16), "seq", scatter_dimension=1, tiled=True
        ).astype(jnp.float32),
        lax.psum_scatter(
            down_part.astype(jnp.bfloat16), "seq", scatter_dimension=1, tiled=True
        ).astype(jnp.float32),
    )
    query_seq, key_seq, value_seq, output_seq, up_seq, down_seq = seq_summed
    query_grad, key_grad, value_grad, output_grad, up_grad, down_grad = (
        lax.psum_scatter(
            query_seq.astype(jnp.bfloat16), "batch", scatter_dimension=0, tiled=True
        ).astype(jnp.float32),
        lax.psum_scatter(
            key_seq.astype(jnp.bfloat16), "batch", scatter_dimension=0, tiled=True
        ).astype(jnp.float32),
        lax.psum_scatter(
            value_seq.astype(jnp.bfloat16), "batch", scatter_dimension=0, tiled=True
        ).astype(jnp.float32),
        lax.psum_scatter(
            output_seq.astype(jnp.bfloat16), "batch", scatter_dimension=0, tiled=True
        ).astype(jnp.float32),
        lax.psum_scatter(
            up_seq.astype(jnp.bfloat16), "batch", scatter_dimension=0, tiled=True
        ).astype(jnp.float32),
        lax.psum_scatter(
            down_seq.astype(jnp.bfloat16), "batch", scatter_dimension=0, tiled=True
        ).astype(jnp.float32),
    )
    compress_grad, first_gain_grad, first_bias_grad, second_gain_grad, second_bias_grad = lax.psum(
        (compress_part, first_gain_part, first_bias_part, second_gain_part, second_bias_part),
        ("batch", "seq"),
    )
    return (
        layer_out,
        input_grad.reshape(set_count, row_count, model_width),
        query_grad,
        key_grad,
        value_grad,
        output_grad,
        up_grad,
        down_grad,
        compress_grad,
        first_gain_grad,
        first_bias_grad,
        second_gain_grad,
        second_bias_grad,
    )


def solution(mesh):
    in_specs = (
        P("batch", "seq", None),
        P("batch", "seq", None),
        P("batch"),
        P("batch", None),
        P(),
        P(),
        P(),
        P(),
        P(),
        P(),
        P(),
        P(),
        P(),
        P(),
        P(),
    )
    out_specs = (
        P("batch", "seq", None),
        P("batch", "seq", None),
        P("batch", "seq"),
        P("batch", "seq"),
        P("batch", "seq"),
        P("batch", "seq"),
        P("batch", "seq"),
        P("batch", "seq"),
        P(),
        P(),
        P(),
        P(),
        P(),
    )
    return jax.shard_map(local, mesh=mesh, in_specs=in_specs, out_specs=out_specs, check_vma=False)
```

profile of v0, /device:TPU:0, one launch (start us, length us, event | category | flops | bytes accessed | tf_op | source)
XLA Modules:
  0.0 1402.0 jit_solution(12386754253375201391)
XLA Ops:
  44.0 246.2 %while.35 = (s32[]{:T(128)}, bf16[4,256,1536]{2,1,0:T(8,128)(2,1)}, f32[4,256,1536]{2,1,0:T(8,128)}, s32[]{:T(128)}, s32[]{:T(128)}, /*index=5*/pred[4]{0:T(512)...) while((s32[]{:T(128)}, bf16[4,256,1536]{2,1,0:T(8,128)(2,1)}, ...), condition=%wide.region_2.3_spmd, body=%wide.region_1.2_spmd.sunk | while | flops 4718627 | bytes 84935176 | solution.py:98
  47.1 70.4 %collective-permute-done = bf16[4,256,1536]{2,1,0:T(8,128)(2,1)} collective-permute-done((bf16[4,256,1536]{2,1,0:T(8,128)(2,1)}, bf16[4,256,1536]{2,1,0:T(8,128)(2,1)}, u32[]{:S(2)}, u32[]{:S(2)}) %collective-permute-start) | collective-permute-done | bytes 3145760 | tf_op jit(solution)/shard_map/while/body/eval_jaxpr/ppermute | solution.py:13
  127.8 71.4 %collective-permute-done = bf16[4,256,1536]{2,1,0:T(8,128)(2,1)} collective-permute-done((bf16[4,256,1536]{2,1,0:T(8,128)(2,1)}, bf16[4,256,1536]{2,1,0:T(8,128)(2,1)}, u32[]{:S(2)}, u32[]{:S(2)}) %collective-permute-start) | collective-permute-done | bytes 3145760 | tf_op jit(solution)/shard_map/while/body/eval_jaxpr/ppermute | solution.py:13
  209.5 70.5 %collective-permute-done = bf16[4,256,1536]{2,1,0:T(8,128)(2,1)} collective-permute-done((bf16[4,256,1536]{2,1,0:T(8,128)(2,1)}, bf16[4,256,1536]{2,1,0:T(8,128)(2,1)}, u32[]{:S(2)}, u32[]{:S(2)}) %collective-permute-start) | collective-permute-done | bytes 3145760 | tf_op jit(solution)/shard_map/while/body/eval_jaxpr/ppermute | solution.py:13
  310.0 13.0 multiply_reduce_fusion.1
  323.0 10.8 exponential_reduce_fusion
  333.9 10.5 convert_bitcast_fusion
  352.1 68.1 %multiply_convert_fusion.1 = (bf16[2048,3072]{1,0:T(8,128)(2,1)}, f32[2048,3072]{1,0:T(8,128)}, f32[2048,3072]{1,0:T(8,128)}) fusion(bf16[768,3072]{1,0:T(8,128)(2,1)S(1)} %bitcast.125, f32[2048,768]{1,0:T(8,128)S(1)} %get-tuple-element.442, f32[768]{0:T(1024)S(1)} %copy-done.42, f32[768]{0:T(1024)S(1)} %copy-done.35, f32[2048]{0:T(1024)S(1)} %fusion.38, ...), kind=kOutput, calls=%fused_computation.11 | convolution fusion | flops 10080485376 | bytes 73947136 | tf_op jit(solution)/shard_map/dot_general | solution.py:119
  420.3 13.6 fusion.56
  443.8 29.7 %add_convert_fusion = bf16[2048,3072]{1,0:T(8,128)(2,1)} fusion(f32[2048,3072]{1,0:T(8,128)} %get-tuple-element.424, f32[2048,3072]{1,0:T(8,128)} %get-tuple-element.443, bf16[3072,768]{1,0:T(8,128)(2,1)} %param.28, f32[2048,768]{1,0:T(8,128)} %get-tuple-element.422, f32[2048]{0:T(1024)S(1)} %negate_multiply_fusion.2), kind=kOutput, calls=%fused_computation.10 | convolution fusion | flops 9754902528 | bytes 73932800 | tf_op jit(solution)/shard_map/dot_general | solution.py:34
  473.6 20.8 %multiply_reduce_fusion.2 = (f32[768]{0:T(1024)}, f32[2048]{0:T(1024)S(1)}, f32[768]{0:T(1024)}, f32[2048,768]{1,0:T(8,128)}) fusion(f32[2048,768]{1,0:T(8,128)} %copy-done.8, f32[2048]{0:T(1024)S(1)} %fusion.38, f32[2048]{0:T(1024)S(1)} %broadcast_multiply_fusion.1, f32[768]{0:T(1024)S(1)} %copy-done.35, bf16[2048,3072]{1,0:T(8,128)(2,1)} %add_convert_fusion, ...), kind=kOutput, calls=%fused_computation.42 | convolution fusion | flops 9679400960 | bytes 36217856 | tf_op jit(solution)/shard_map/dot_general | solution.py:34
  517.8 13.4 fusion.19
  531.2 16.9 %multiply_reduce_fusion = (f32[4,12,512]{2,1,0:T(8,128)S(1)}, f32[4,12,512,256]{2,3,1,0:T(8,128)}) fusion(f32[4,12,512,256]{2,3,1,0:T(8,128)} %get-tuple-element.440, f32[4,12,512]{2,1,0:T(8,128)S(1)} %copy-done.20, bf16[4,256,12,64]{1,3,2,0:T(8,128)(2,1)S(1)} %bitcast.114, bf16[4,512,12,64]{1,0,3,2:T(4,128)(2,1)} %reshape.164), kind=kOutput, calls=%fused_computation.9 | convolution fusion | flops 830447616 | bytes 55246848 | tf_op jit(solution)/shard_map/srhd,skhd->shrk/dot_general | solution.py:142
  551.6 21.6 %multiply_convert_fusion = bf16[4,12,512,256]{2,3,1,0:T(8,128)(2,1)} fusion(f32[4,12,512,256]{2,3,1,0:T(8,128)} %get-tuple-element.448, f32[4,12,512,256]{2,3,1,0:T(8,128)} %get-tuple-element.440, f32[4,12,512]{2,1,0:T(8,128)S(1)} %get-tuple-element.447, f32[4,12,512]{2,1,0:T(8,128)S(1)} %copy-done.20), kind=kLoop, calls=%fused_computation.8 | loop fusion | flops 31457280 | bytes 63111168 | tf_op jit(solution)/shard_map/convert_element_type | solution.py:146
  605.0 228.5 %while.36 = (s32[]{:T(128)}, bf16[4,256,1536]{2,1,0:T(8,128)(2,1)}, f32[4,256,1536]{2,1,0:T(8,128)}, s32[]{:T(128)}, s32[]{:T(128)}, /*index=5*/pred[4]{0:T(512)...) while((s32[]{:T(128)}, bf16[4,256,1536]{2,1,0:T(8,128)(2,1)}, ...), condition=%wide.region_15.16_spmd, body=%wide.region_14.15_spmd.sunk | while | flops 6291491 | bytes 31457756 | solution.py:173
  605.1 67.7 %collective-permute-done.1 = bf16[4,256,1536]{2,1,0:T(8,128)(2,1)} collective-permute-done((bf16[4,256,1536]{2,1,0:T(8,128)(2,1)}, bf16[4,256,1536]{2,1,0:T(8,128)(2,1)}, u32[]{:S(2)}, u32[]{:S(2)}) %collective-permute-start.1) | collective-permute-done | bytes 3145760 | tf_op jit(solution)/shard_map/while/body/eval_jaxpr/ppermute | solution.py:13
  683.5 64.7 %collective-permute-done.1 = bf16[4,256,1536]{2,1,0:T(8,128)(2,1)} collective-permute-done((bf16[4,256,1536]{2,1,0:T(8,128)(2,1)}, bf16[4,256,1536]{2,1,0:T(8,128)(2,1)}, u32[]{:S(2)}, u32[]{:S(2)}) %collective-permute-start.1) | collective-permute-done | bytes 3145760 | tf_op jit(solution)/shard_map/while/body/eval_jaxpr/ppermute | solution.py:13
  761.1 63.7 %collective-permute-done.1 = bf16[4,256,1536]{2,1,0:T(8,128)(2,1)} collective-permute-done((bf16[4,256,1536]{2,1,0:T(8,128)(2,1)}, bf16[4,256,1536]{2,1,0:T(8,128)(2,1)}, u32[]{:S(2)}, u32[]{:S(2)}) %collective-permute-start.1) | collective-permute-done | bytes 3145760 | tf_op jit(solution)/shard_map/while/body/eval_jaxpr/ppermute | solution.py:13
  850.6 11.8 fusion.17
  873.5 16.8 %convolution_convert_fusion.2 = bf16[3072,768]{0,1:T(8,128)(2,1)} fusion(bf16[2048,3072]{1,0:T(8,128)(2,1)} %get-tuple-element.423, f32[2048,768]{1,0:T(8,128)} %get-tuple-element.422, f32[2048]{0:T(1024)S(1)} %negate_multiply_fusion.2), kind=kOutput, calls=%fused_computation.59 | convolution fusion | flops 9669181440 | bytes 23601152 | tf_op jit(solution)/shard_map/dot_general | solution.py:28
  890.4 18.1 %convolution_convert_fusion.3 = bf16[768,3072]{1,0:T(8,128)(2,1)} fusion(bf16[2048,3072]{1,0:T(8,128)(2,1)} %add_convert_fusion, f32[2048,768]{1,0:T(8,128)} %copy-done.8, f32[768]{0:T(1024)S(1)} %copy-done.43, f32[768]{0:T(1024)S(1)} %copy-done.36, f32[2048]{0:T(1024)S(1)} %copy-done.28, f32[2048]{0:T(1024)S(1)} %copy-done.24), kind=kOutput, calls=%fused_computation.60 | convolution fusion | flops 9673900032 | bytes 23615488 | tf_op jit(solution)/shard_map/dot_general | solution.py:28
  910.5 14.0 reduce-scatter.25.cloned.1.call-done
  926.4 28.9 %reduce-scatter.27.cloned.1.call-done = bf16[768,192]{0,1:T(8,128)(2,1)} async-done(((bf16[768,768]{0,1:T(8,128)(2,1)}), bf16[768,192]{0,1:T(8,128)(2,1)}) %reduce-scatter.27.cloned.1.call-update) | async-done | bytes 294928 | tf_op jit(solution)/shard_map/reduce_scatter | solution.py:206
  957.3 28.1 %reduce-scatter.29.cloned.1.call-done = bf16[768,192]{0,1:T(8,128)(2,1)} async-done(((bf16[768,768]{0,1:T(8,128)(2,1)}), bf16[768,192]{0,1:T(8,128)(2,1)}) %reduce-scatter.29.cloned.1.call-update) | async-done | bytes 294928 | tf_op jit(solution)/shard_map/reduce_scatter | solution.py:209
  987.4 84.2 %reduce-scatter.35.cloned.1.call-done = bf16[3072,192]{0,1:T(8,128)(2,1)} async-done(((bf16[3072,768]{0,1:T(8,128)(2,1)}), bf16[3072,192]{0,1:T(8,128)(2,1)}) %reduce-scatter.35.cloned.1.call-update) | async-done | bytes 1179664 | tf_op jit(solution)/shard_map/reduce_scatter | solution.py:215
  1074.1 85.4 %reduce-scatter.31.cloned.1.call-done = bf16[768,768]{1,0:T(8,128)(2,1)} async-done(((bf16[768,3072]{1,0:T(8,128)(2,1)}), bf16[768,768]{1,0:T(8,128)(2,1)}) %reduce-scatter.31.cloned.1.call-update) | async-done | bytes 1179664 | tf_op jit(solution)/shard_map/reduce_scatter | solution.py:212
  1196.5 13.9 add_add_fusion.2
  1210.9 41.9 %all-reduce.1 = (f32[768]{0:T(1024)}, f32[768]{0:T(1024)}, f32[768]{0:T(1024)}, f32[768]{0:T(1024)}) all-reduce(f32[768]{0:T(1024)S(1)} %copy-done.33, f32[768]{0:T(1024)S(1)} %copy-done.34, f32[768]{0:T(1024)S(1)} %copy-done.30, f32[768]{0:T(1024)S(1)} %convert_reduce_fusion), channel_id=1, replica_groups=mesh['batch'=8,'seq'=4] {'batch','seq'}, use_global_device_ids=true, to_apply=%region_30.31 | all-reduce | flops 3072 | bytes 24576 | tf_op jit(solution)/shard_map/psum | solution.py:240
  1256.1 14.8 %reduce-scatter.41.cloned.1.call-done = bf16[96,192]{1,0:T(8,128)(2,1)} async-done(((bf16[768,192]{1,0:T(8,128)(2,1)}), bf16[96,192]{1,0:T(8,128)(2,1)}) %reduce-scatter.41.cloned.1.call-update) | async-done | bytes 36880
  1272.6 35.1 %reduce-scatter.43.cloned.1.call-done = bf16[96,192]{1,0:T(8,128)(2,1)} async-done(((bf16[768,192]{1,0:T(8,128)(2,1)}), bf16[96,192]{1,0:T(8,128)(2,1)}) %reduce-scatter.43.cloned.1.call-update) | async-done | bytes 36880
  1309.4 40.2 %reduce-scatter.45.cloned.1.call-done = bf16[384,192]{1,0:T(8,128)(2,1)} async-done(((bf16[3072,192]{1,0:T(8,128)(2,1)}), bf16[384,192]{1,0:T(8,128)(2,1)}) %reduce-scatter.45.cloned.1.call-update) | async-done | bytes 147472
  1351.4 38.1 %reduce-scatter.33.cloned.1.call-done = bf16[96,768]{1,0:T(8,128)(2,1)} async-done(((bf16[768,768]{1,0:T(8,128)(2,1)}), bf16[96,768]{1,0:T(8,128)(2,1)}) %reduce-scatter.33.cloned.1.call-update) | async-done | bytes 147472 | tf_op jit(solution)/shard_map/reduce_scatter | solution.py:233
  (249 shorter events, 288.3 us)
Async XLA Ops:
  8.0 340.0 %copy-start = (bf16[768,768]{1,0:T(8,128)(2,1)S(1)}, bf16[768,768]{1,0:T(8,128)(2,1)}, u32[]{:S(2)}) copy-start(bf16[768,768]{1,0:T(8,128)(2,1)} %param.26) | copy-start | bytes 3538948
  8.0 900.5 %reduce-scatter.23.cloned.1.call-start = ((), (), s32[]{:S(2)}) async-start(), calls=%async_computation.12 | async-start | bytes 1474560 | tf_op jit(solution)/shard_map/reduce_scatter | solution.py:200
  44.0 73.5 %collective-permute-start = (bf16[4,256,1536]{2,1,0:T(8,128)(2,1)}, bf16[4,256,1536]{2,1,0:T(8,128)(2,1)}, u32[]{:S(2)}, u32[]{:S(2)}) collective-permute-start(bf16[4,256,1536]{2,1,0:T(8,128)(2,1)} %get-tuple-element.584), channel_id=1, source_target_pairs={{3,0},{0,1},{1,2},{2,3},{7,4},{4,5},{5,6},{6,7},{11,8},{8,9},{9,10... | collective-permute-start | bytes 9437192 | tf_op jit(solution)/shard_map/while/body/eval_jaxpr/ppermute | solution.py:13
  47.1 74.2 %copy-start.1 = (f32[4,256,1536]{2,1,0:T(8,128)S(1)}, f32[4,256,1536]{2,1,0:T(8,128)}, u32[]{:S(2)}) copy-start(f32[4,256,1536]{2,1,0:T(8,128)} %get-tuple-element.585) | copy-start | bytes 18874372 | tf_op jit(solution)/shard_map/while
  127.8 71.4 %collective-permute-start = (bf16[4,256,1536]{2,1,0:T(8,128)(2,1)}, bf16[4,256,1536]{2,1,0:T(8,128)(2,1)}, u32[]{:S(2)}, u32[]{:S(2)}) collective-permute-start(bf16[4,256,1536]{2,1,0:T(8,128)(2,1)} %get-tuple-element.584), channel_id=1, source_target_pairs={{3,0},{0,1},{1,2},{2,3},{7,4},{4,5},{5,6},{6,7},{11,8},{8,9},{9,10... | collective-permute-start | bytes 9437192 | tf_op jit(solution)/shard_map/while/body/eval_jaxpr/ppermute | solution.py:13
  127.8 75.2 %copy-start.1 = (f32[4,256,1536]{2,1,0:T(8,128)S(1)}, f32[4,256,1536]{2,1,0:T(8,128)}, u32[]{:S(2)}) copy-start(f32[4,256,1536]{2,1,0:T(8,128)} %get-tuple-element.585) | copy-start | bytes 18874372 | tf_op jit(solution)/shard_map/while
  209.5 70.5 %collective-permute-start = (bf16[4,256,1536]{2,1,0:T(8,128)(2,1)}, bf16[4,256,1536]{2,1,0:T(8,128)(2,1)}, u32[]{:S(2)}, u32[]{:S(2)}) collective-permute-start(bf16[4,256,1536]{2,1,0:T(8,128)(2,1)} %get-tuple-element.584), channel_id=1, source_target_pairs={{3,0},{0,1},{1,2},{2,3},{7,4},{4,5},{5,6},{6,7},{11,8},{8,9},{9,10... | collective-permute-start | bytes 9437192 | tf_op jit(solution)/shard_map/while/body/eval_jaxpr/ppermute | solution.py:13
  209.5 74.2 %copy-start.1 = (f32[4,256,1536]{2,1,0:T(8,128)S(1)}, f32[4,256,1536]{2,1,0:T(8,128)}, u32[]{:S(2)}) copy-start(f32[4,256,1536]{2,1,0:T(8,128)} %get-tuple-element.585) | copy-start | bytes 18874372 | tf_op jit(solution)/shard_map/while
  351.1 69.2 %copy-start.8 = (f32[2048,768]{1,0:T(8,128)}, f32[2048,768]{1,0:T(8,128)S(1)}, u32[]{:S(2)}) copy-start(f32[2048,768]{1,0:T(8,128)S(1)} %get-tuple-element.442) | copy-start | bytes 18874372
  351.1 143.2 %copy-start.23 = (f32[2048]{0:T(1024)}, f32[2048]{0:T(1024)S(1)}, u32[]{:S(2)}) copy-start(f32[2048]{0:T(1024)S(1)} %broadcast_multiply_fusion.1) | copy-start | bytes 24580
  352.0 68.2 %copy-start.25 = (f32[2048]{0:T(1024)}, f32[2048]{0:T(1024)S(1)}, u32[]{:S(2)}) copy-start(f32[2048]{0:T(1024)S(1)} %multiply_reduce_fusion.5) | copy-start | bytes 24580
  352.1 142.3 %copy-start.27 = (f32[2048]{0:T(1024)}, f32[2048]{0:T(1024)S(1)}, u32[]{:S(2)}) copy-start(f32[2048]{0:T(1024)S(1)} %fusion.38) | copy-start | bytes 24580
  352.1 68.2 %copy-start.39 = (bf16[3072,768]{1,0:T(8,128)(2,1)S(1)}, bf16[3072,768]{1,0:T(8,128)(2,1)}, u32[]{:S(2)}) copy-start(bf16[3072,768]{1,0:T(8,128)(2,1)} %param.28) | copy-start | bytes 14155780
  473.6 20.8 %copy-start.26 = (f32[2048]{0:T(1024)S(1)}, f32[2048]{0:T(1024)}, u32[]{:S(2)}) copy-start(f32[2048]{0:T(1024)} %copy-done.25) | copy-start | bytes 24580
  551.6 21.6 %copy-start.3 = (bf16[4,512,12,64]{1,0,3,2:T(4,128)(2,1)S(1)}, bf16[4,512,12,64]{1,0,3,2:T(4,128)(2,1)}, u32[]{:S(2)}) copy-start(bf16[4,512,12,64]{1,0,3,2:T(4,128)(2,1)} %reshape.161) | copy-start | bytes 9437188
  605.0 228.5 %copy-start.18 = (bf16[4,512,256]{2,1,0:T(8,128)(2,1)S(1)}, bf16[4,512,256]{2,1,0:T(8,128)(2,1)}, u32[]{:S(2)}) copy-start(bf16[4,512,256]{2,1,0:T(8,128)(2,1)} %copy-done.17) | copy-start | bytes 3145732
  605.0 67.8 %collective-permute-start.1 = (bf16[4,256,1536]{2,1,0:T(8,128)(2,1)}, bf16[4,256,1536]{2,1,0:T(8,128)(2,1)}, u32[]{:S(2)}, u32[]{:S(2)}) collective-permute-start(bf16[4,256,1536]{2,1,0:T(8,128)(2,1)} %get-tuple-element.626), channel_id=1, source_target_pairs={{1,0},{2,1},{3,2},{0,3},{5,4},{6,5},{7,6},{4,7},{9,8},{10,9},{11,1... | collective-permute-start | bytes 9437192 | tf_op jit(solution)/shard_map/while/body/eval_jaxpr/ppermute | solution.py:13
  681.4 66.8 %collective-permute-start.1 = (bf16[4,256,1536]{2,1,0:T(8,128)(2,1)}, bf16[4,256,1536]{2,1,0:T(8,128)(2,1)}, u32[]{:S(2)}, u32[]{:S(2)}) collective-permute-start(bf16[4,256,1536]{2,1,0:T(8,128)(2,1)} %get-tuple-element.626), channel_id=1, source_target_pairs={{1,0},{2,1},{3,2},{0,3},{5,4},{6,5},{7,6},{4,7},{9,8},{10,9},{11,1... | collective-permute-start | bytes 9437192 | tf_op jit(solution)/shard_map/while/body/eval_jaxpr/ppermute | solution.py:13
  756.9 67.9 %collective-permute-start.1 = (bf16[4,256,1536]{2,1,0:T(8,128)(2,1)}, bf16[4,256,1536]{2,1,0:T(8,128)(2,1)}, u32[]{:S(2)}, u32[]{:S(2)}) collective-permute-start(bf16[4,256,1536]{2,1,0:T(8,128)(2,1)} %get-tuple-element.626), channel_id=1, source_target_pairs={{1,0},{2,1},{3,2},{0,3},{5,4},{6,5},{7,6},{4,7},{9,8},{10,9},{11,1... | collective-permute-start | bytes 9437192 | tf_op jit(solution)/shard_map/while/body/eval_jaxpr/ppermute | solution.py:13
  864.3 60.2 %reduce-scatter.25.cloned.1.call-start = ((), (), s32[]{:S(2)}) async-start(), calls=%async_computation.13 | async-start | bytes 1474560 | tf_op jit(solution)/shard_map/reduce_scatter | solution.py:203
  865.0 90.3 %reduce-scatter.27.cloned.1.call-start = ((), (), s32[]{:S(2)}) async-start(), calls=%async_computation.14 | async-start | bytes 1474560 | tf_op jit(solution)/shard_map/reduce_scatter | solution.py:206
  865.8 119.6 %reduce-scatter.29.cloned.1.call-start = ((), (), s32[]{:S(2)}) async-start(), calls=%async_computation.15 | async-start | bytes 1474560 | tf_op jit(solution)/shard_map/reduce_scatter | solution.py:209
  873.4 198.1 %reduce-scatter.35.cloned.1.call-start = ((), (), s32[]{:S(2)}) async-start(), calls=%async_computation.18 | async-start | bytes 5898240 | tf_op jit(solution)/shard_map/reduce_scatter | solution.py:215
  890.3 269.3 %reduce-scatter.31.cloned.1.call-start = ((), (), s32[]{:S(2)}) async-start(), calls=%async_computation.16 | async-start | bytes 5898240 | tf_op jit(solution)/shard_map/reduce_scatter | solution.py:212
  908.4 251.4 %copy-start.31 = (s32[4]{0:T(128)S(1)}, s32[4]{0:T(128)}, u32[]{:S(2)}) copy-start(s32[4]{0:T(128)} %get-tuple-element.426) | copy-start | bytes 52
  908.4 344.3 %reduce-scatter.37.cloned.1.call-start = ((), (), s32[]{:S(2)}) async-start(), calls=%async_computation.20 | async-start | bytes 442368
  910.4 344.0 %reduce-scatter.39.cloned.1.call-start = ((), (), s32[]{:S(2)}) async-start(), calls=%async_computation.21 | async-start | bytes 442368
  926.4 344.5 %reduce-scatter.41.cloned.1.call-start = ((), (), s32[]{:S(2)}) async-start(), calls=%async_computation.22 | async-start | bytes 442368
  957.2 350.5 %reduce-scatter.43.cloned.1.call-start = ((), (), s32[]{:S(2)}) async-start(), calls=%async_computation.23 | async-start | bytes 442368
  987.3 362.3 %reduce-scatter.45.cloned.1.call-start = ((), (), s32[]{:S(2)}) async-start(), calls=%async_computation.24 | async-start | bytes 1769472
  1074.1 315.4 %reduce-scatter.33.cloned.1.call-start = ((), (), s32[]{:S(2)}) async-start(), calls=%async_computation.17 | async-start | bytes 1327104 | tf_op jit(solution)/shard_map/reduce_scatter | solution.py:233
  1159.5 231.5 %all-reduce.4.cloned.1.call-start = ((), (), s32[]{:S(2)}) async-start(), calls=%async_computation.19 | async-start | bytes 4194304 | tf_op jit(solution)/shard_map/psum | solution.py:240
  (39 other events, 275.7 us)
Sparse Core Ops, SparseCore 0:
  864.4 29.8 reduce-scatter.22
  896.6 27.8 reduce-scatter.24
  927.4 27.8 reduce-scatter.26
  957.5 27.8 reduce-scatter.28
  987.5 83.9 reduce-scatter.34
  1073.7 85.7 reduce-scatter.30
  1162.6 34.3 reduce-scatter.36
  1200.0 33.8 reduce-scatter.38
  1237.0 33.8 reduce-scatter.40
  1273.8 33.8 reduce-scatter.42
  1311.0 38.5 reduce-scatter.44
  1352.7 36.7 reduce-scatter.32
Sparse Core Ops, SparseCore 1:
  1196.5 134.8 all-reduce.3
where the time goes:
time: 1410 us; the launch traced here: 1400 us
  waiting for transfers between devices  779 us (55%)
  matrix products  311 us (22%)
  local copies, waits for them, and re-layouts  129 us (9%)
  other arithmetic  107 us (8%)
  blocking collectives  41.9 us (3%)
  between operations  24.6 us (2%)
    ppermute x6, waiting for transfers between devices, shifted(): return lax.ppermute(block, axis, route)  408 us
    unnamed x18, waiting for transfers between devices  91.7 us
    reduce_scatter x1, waiting for transfers between devices, local(): lax.psum_scatter(up_part.astype(jnp.bfloat16), 'seq', scatter_dimension=1...  85.4 us
    reduce_scatter x1, waiting for transfers between devices, local(): lax.psum_scatter(down_part.astype(jnp.bfloat16), 'seq', scatter_dimension...  84.2 us
    dot_general x4, matrix products, contract_cols(): lax.dot_general(left_in, right_in, (((1,), (1,)), ((), ())), preferred_el...  68.5 us
    dot_general x1, matrix products, local(): upward = jnp.dot(hidden_low, up_w, preferred_element_type=jnp.float32)  68.1 us
    dot_general x4, matrix products, contract_rows(): lax.dot_general(left_in, right_in, (((0,), (0,)), ((), ())), preferred_el...  54.1 us
    psum x1, blocking collectives, local(): lax.psum((compress_part, first_gain_part, first_bias_part, second_gain_pa...  41.9 us
  transfers between devices with their start and end apart: 19, of which 15 were waited for; matrix products, arithmetic and copies ran while one was open for 7% of the time, Pallas kernels for 0%

commit v1 on v0

v1 whole, which is shorter than its diff:
```python
import functools

import jax
import jax.numpy as jnp
from jax import lax
from jax.experimental import pallas as pl
from jax.experimental.pallas import tpu as pltpu
from jax.sharding import PartitionSpec as P

DH = 64
LANES = 128
TILE = 8
SCALE = DH ** (-0.5)
EPS = 1e-05
MESH = pl.DeviceIdType.MESH
VMEM_LIMIT = 63 * 1024 * 1024
bf16 = jnp.bfloat16
f32 = jnp.float32


def dot(left, right):
    return lax.dot_general(left, right, (((1,), (0,)), ((), ())), preferred_element_type=f32)


def dot_nt(left, right):
    return lax.dot_general(left, right, (((1,), (1,)), ((), ())), preferred_element_type=f32)


def dot_tn(left, right):
    return lax.dot_general(left, right, (((0,), (0,)), ((), ())), preferred_element_type=f32)


def params(**more):
    return pltpu.CompilerParams(vmem_limit_bytes=VMEM_LIMIT, **more)


def whole(shape):
    return pl.BlockSpec(shape, lambda *_: (0,) * len(shape), pipeline_mode=pl.Buffered(1))


def per_set(shape):
    return pl.BlockSpec((1,) + tuple(shape), lambda s, *_: (s,) + (0,) * len(shape))


def aligned(start):
    begin = start // TILE * TILE
    return pl.multiple_of(begin, TILE), start - begin


def place():
    batch = lax.axis_index("batch")
    return batch // 4, batch // 2 % 2, batch % 2, lax.axis_index("seq")


def device(y, x, core, z):
    return ((y * 2 + x) * 2 + core, z)


def greet(others):
    barrier = pltpu.get_barrier_semaphore()
    for other in others:
        pl.semaphore_signal(barrier, inc=1, device_id=other, device_id_type=MESH)
    pl.semaphore_wait(barrier, len(others))


def remote(src, dst, send_sem, recv_sem, target):
    return pltpu.make_async_remote_copy(src, dst, send_sem, recv_sem, device_id=target, device_id_type=MESH)


class LineSum:
    lag = 2

    def __init__(self, line, own, from_left, from_right, to_right, to_left, sems):
        y, x, core, self.z = place()
        self.line = line
        self.own = own
        right, left = device(y, x, core, (self.z + 1) % line), device(y, x, core, (self.z + line - 1) % line)
        self.ways = (
            (from_left, to_right, right, self.z > 0, self.z < line - 1, sems[0], sems[1]),
            (from_right, to_left, left, self.z < line - 1, self.z > 0, sems[2], sems[3]),
        )

    def prepare(self):
        for arrived, _, _, has_before, _, _, _ in self.ways:

            @pl.when(jnp.logical_not(has_before))
            def _():
                arrived[...] = jnp.zeros_like(arrived)

    def copy(self, way, at):
        arrived, leaving, target, _, _, send, recv = way
        return remote(leaving.at[at], arrived.at[at], send.at[at], recv.at[at], target)

    def forward(self, way, at):
        arrived, leaving, _, has_before, has_after, _, _ = way

        @pl.when(has_before)
        def _():
            self.copy(way, at).wait_recv()

        leaving[at] = arrived[at] + self.own[at]

        @pl.when(has_after)
        def _():
            self.copy(way, at).start()

    def slots(self):
        return self.own.shape[0] + self.lag * (self.line - 1)

    def serve(self, slot):
        for way, hops in zip(self.ways, (self.z, self.line - 1 - self.z)):
            at = slot - self.lag * hops

            @pl.when(jnp.logical_and(at >= 0, at < self.own.shape[0]))
            def _():
                self.forward(way, at)

    def total(self, at, joined):
        left, right = self.ways[0][0][at].astype(f32), self.ways[1][0][at].astype(f32)
        return (self.own[at].astype(f32) + jnp.where(joined, left + right, 0.0)).astype(bf16)

    def finish(self, at):
        for way in self.ways:

            @pl.when(way[4])
            def _():
                self.copy(way, at).wait_send()


def line_sum_kernel(line, own_ref, long_ref, out_ref, from_left, from_right, to_right, to_left, *sems):
    y, x, core, z = place()
    barrier = pltpu.get_barrier_semaphore()
    for there, other in ((z > 0, z - 1), (z < line - 1, z + 1)):

        @pl.when(there)
        def _():
            pl.semaphore_signal(barrier, inc=1, device_id=device(y, x, core, other), device_id_type=MESH)

    both = jnp.logical_and(z > 0, z < line - 1).astype(jnp.int32)
    pl.semaphore_wait(barrier, 1 + both)
    sums = LineSum(line, own_ref, from_left, from_right, to_right, to_left, sems)
    sums.prepare()
    count = own_ref.shape[0]

    def slot(at, carry):
        sums.serve(at)
        return carry

    lax.fori_loop(0, sums.slots(), slot, 0)
    for at in range(count):
        out_ref[at] = sums.total(at, long_ref[at * long_ref.shape[0] // count] > 0)
        sums.finish(at)


def line_sum(part, set_kind, identity):
    sets, rows, width = part.shape
    pieces = 4
    split = part.reshape(sets * pieces, rows // pieces, width)
    line = lax.axis_size("seq")
    vmem = pl.BlockSpec(memory_space=pltpu.VMEM)
    out = pl.pallas_call(
        functools.partial(line_sum_kernel, line),
        in_specs=[vmem, pl.BlockSpec(memory_space=pltpu.SMEM)],
        out_specs=vmem,
        out_shape=jax.ShapeDtypeStruct(split.shape, bf16),
        scratch_shapes=[pltpu.VMEM(split.shape, bf16)] * 4 + [pltpu.SemaphoreType.DMA((sets * pieces,))] * 4,
        compiler_params=params(collective_id=identity, has_side_effects=True),
        name="line_sum",
    )(split, set_kind)
    return out.reshape(part.shape)


class Scatter:
    def __init__(self, x_first, part, from_core, from_first, from_second, send, recv):
        y, x, core, z = place()
        self.part, self.recvs = part, (from_core, from_first, from_second)
        along_x, along_y = device(y, 1 - x, core, z), device(1 - y, x, core, z)
        self.core, self.x, self.y, self.x_first = core, x, y, x_first
        if x_first:
            sources = (part.at[:, :, 1 - core], from_core.at[:, 1 - x], from_first.at[1 - y])
            targets = (device(y, x, 1 - core, z), along_x, along_y)
        else:
            sources = (part.at[:, :, 1 - core], from_core.at[1 - y], from_first.at[1 - x])
            targets = (device(y, x, 1 - core, z), along_y, along_x)
        self.copies = [
            remote(sources[i], self.recvs[i], send.at[i], recv.at[i], targets[i]) for i in range(3)
        ]

    def start(self):
        self.copies[0].start()

    def first(self):
        self.copies[0].wait_recv()
        self.recvs[0][...] = self.recvs[0][...] + self.part[:, :, self.core]
        self.copies[1].start()

    def second(self):
        self.copies[1].wait_recv()
        kept = self.recvs[0][:, self.x] if self.x_first else self.recvs[0][self.y]
        self.recvs[1][...] = self.recvs[1][...] + kept
        self.copies[2].start()

    def done(self):
        self.copies[2].wait_recv()
        kept = self.recvs[1][self.y] if self.x_first else self.recvs[1][self.x]
        return self.recvs[2][...].astype(f32) + kept.astype(f32)

    def finish(self):
        for copy in self.copies:
            copy.wait_send()


class LineScatter:
    def __init__(self, line, blocks, arrived, send, recv):
        y, x, core, self.z = place()
        self.blocks, self.arrived, self.line = blocks, arrived, line
        self.copies = []
        for d in range(1, line):
            to = (self.z + d) % line
            self.copies.append(
                remote(blocks.at[to], arrived.at[d - 1], send.at[d - 1], recv.at[d - 1], device(y, x, core, to))
            )

    def start(self):
        for copy in self.copies:
            copy.start()

    def done(self):
        total = self.blocks[self.z].astype(f32)
        for d, copy in enumerate(self.copies):
            copy.wait_recv()
            total = total + self.arrived[d].astype(f32)
        return total

    def finish(self):
        for copy in self.copies:
            copy.wait_send()


def line_scatter_blocks(blocks, rows, line):
    step = rows.shape[1] // line
    for z in range(line):
        mine = rows[:, z * step : (z + 1) * step]
        if step % LANES:
            top = rows.shape[0] // 2
            mine = jnp.concatenate([mine[:top], mine[top:]], axis=1)
        blocks[z] = mine.astype(bf16)


def scatter_kernel(line, query, key, value, output, up, down, query_out, key_out, value_out, output_out, up_out, down_out, *scratch):
    y, x, core, z = place()
    greet(
        [device(y, x, 1 - core, z), device(y, 1 - x, core, z), device(1 - y, x, core, z)]
        + [device(y, x, core, (z + d) % line) for d in range(1, line)]
    )
    scratch = list(scratch)
    take = lambda n: [scratch.pop(0) for _ in range(n)]
    jobs = []
    for i, (part, out) in enumerate(
        ((up, up_out), (down, down_out), (output, output_out), (query, query_out), (key, key_out), (value, value_out))
    ):
        job = Scatter(i % 2 == 0, part, *take(3), *take(2))
        jobs.append((job, LineScatter(line, *take(4)), out))
    for job, _, _ in jobs:
        job.start()
    for job, _, _ in jobs:
        job.first()
    for job, _, _ in jobs:
        job.second()
    for job, across, _ in jobs:
        line_scatter_blocks(across.blocks, job.done(), line)
        across.start()
    for job, across, out in jobs:
        total = across.done()
        if total.shape != out.shape:
            top, step = total.shape[0], total.shape[1] // 2
            out[:top, :] = total[:, :step]
            out[top:, :] = total[:, step:]
        else:
            out[...] = total
        job.finish()
        across.finish()


def scatter(query, key, value, output, up, down):
    line = lax.axis_size("seq")
    grads = (query, key, value, output, up, down)
    blocked = [v.reshape(2, 2, 2, v.shape[0] // 8, v.shape[1]) for v in grads]
    vmem = pl.BlockSpec(memory_space=pltpu.VMEM)
    scratch = []
    for v in (up, down, output, query, key, value):
        rows, width = v.shape[0] // 8, v.shape[1]
        step = width // line
        block = (rows, step) if step % LANES == 0 else (rows // 2, step * 2)
        scratch += [
            pltpu.VMEM((2, 2, rows, width), bf16),
            pltpu.VMEM((2, rows, width), bf16),
            pltpu.VMEM((rows, width), bf16),
            pltpu.SemaphoreType.DMA((3,)),
            pltpu.SemaphoreType.DMA((3,)),
            pltpu.VMEM((line,) + block, bf16),
            pltpu.VMEM((line - 1,) + block, bf16),
            pltpu.SemaphoreType.DMA((line - 1,)),
            pltpu.SemaphoreType.DMA((line - 1,)),
        ]
    return pl.pallas_call(
        functools.partial(scatter_kernel, line),
        in_specs=[vmem] * 6,
        out_specs=[vmem] * 6,
        out_shape=[jax.ShapeDtypeStruct((v.shape[0] // 8, v.shape[1] // line), f32) for v in grads],
        scratch_shapes=scratch,
        compiler_params=params(collective_id=2, has_side_effects=True),
        name="scatter",
    )(*blocked)


def total_kernel(line, table_ref, norms_ref, table_out, norms_out, mine, from_core, from_plane, from_line, gathered,
                 core_norms, plane_norms, line_norms, *sems):
    y, x, core, z = place()
    plane = y * 2 + x
    sems = list(sems)
    take = lambda: (sems.pop(0), sems.pop(0))
    other = device(y, x, 1 - core, z)
    places = [((y + dy) % 2, (x + dx) % 2) for dy, dx in ((0, 1), (1, 0), (1, 1))]
    planes = [(py * 2 + px, device(py, px, core, z)) for py, px in places]
    lines = [((z + d) % line, device(y, x, core, (z + d) % line)) for d in range(1, line)]
    greet([other] + [to for _, to in planes] + [to for _, to in lines])

    def run(copies):
        for copy in copies:
            copy.start()
        for copy in copies:
            copy.wait()

    rows = mine.shape[-2]
    mine[...] = table_ref[...].astype(bf16)
    core_norms[0] = norms_ref[...]
    s, r = take()
    run([
        remote(mine.at[1 - core], from_core, s.at[0], r.at[0], other),
        remote(core_norms.at[0], core_norms.at[1], s.at[1], r.at[1], other),
    ])
    from_core[...] = from_core[...] + mine[core]
    plane_norms[plane] = core_norms[0] + core_norms[1]
    s, r = take()
    run([remote(from_core.at[p], from_plane.at[i], s.at[i], r.at[i], to) for i, (p, to) in enumerate(planes)]
        + [remote(plane_norms.at[plane], plane_norms.at[plane], s.at[3 + i], r.at[3 + i], to) for i, (_, to) in enumerate(planes)])
    total = from_core[plane].astype(f32)
    for i in range(3):
        total = total + from_plane[i].astype(f32)
    mine[0, 0] = total.astype(bf16)
    line_norms[z] = plane_norms[0] + plane_norms[1] + plane_norms[2] + plane_norms[3]
    s, r = take()
    run([remote(mine.at[0, 0, p], from_line.at[i], s.at[i], r.at[i], to) for i, (p, to) in enumerate(lines)]
        + [remote(line_norms.at[z], line_norms.at[z], s.at[line - 1 + i], r.at[line - 1 + i], to) for i, (_, to) in enumerate(lines)])
    total = mine[0, 0, z].astype(f32)
    for i in range(line - 1):
        total = total + from_line[i].astype(f32)
    gathered[core, plane, z] = total.astype(bf16)
    all_norms = line_norms[0]
    for i in range(1, line):
        all_norms = all_norms + line_norms[i]
    norms_out[...] = all_norms
    s, r = take()
    block = gathered.at[core, plane, z]
    run([remote(block, block, s.at[i], r.at[i], to) for i, (_, to) in enumerate(lines)])
    s, r = take()
    block = gathered.at[core, plane]
    run([remote(block, block, s.at[i], r.at[i], to) for i, (_, to) in enumerate(planes)])
    s, r = take()
    block = gathered.at[core]
    run([remote(block, block, s.at[0], r.at[0], other)])
    table_out[...] = gathered[...].astype(f32)


def total_sum(table, norms):
    line = lax.axis_size("seq")
    longest, comp = table.shape
    rows = longest // (8 * line)
    shape = (2, 4, line, rows, comp)
    vmem = pl.BlockSpec(memory_space=pltpu.VMEM)
    counts = (2, 6, 2 * (line - 1), line - 1, 3, 1)
    out, sums = pl.pallas_call(
        functools.partial(total_kernel, line),
        in_specs=[vmem] * 2,
        out_specs=[vmem] * 2,
        out_shape=[jax.ShapeDtypeStruct(shape, f32), jax.ShapeDtypeStruct(norms.shape, f32)],
        scratch_shapes=[
            pltpu.VMEM(shape, bf16),
            pltpu.VMEM(shape[1:], bf16),
            pltpu.VMEM((3,) + shape[2:], bf16),
            pltpu.VMEM((line - 1,) + shape[3:], bf16),
            pltpu.VMEM(shape, bf16),
            pltpu.VMEM((2,) + norms.shape, f32),
            pltpu.VMEM((4,) + norms.shape, f32),
            pltpu.VMEM((line,) + norms.shape, f32),
        ]
        + [pltpu.SemaphoreType.DMA((n,)) for n in counts for _ in range(2)],
        compiler_params=params(collective_id=3, has_side_effects=True),
        name="total_sum",
    )(table.reshape(shape), norms)
    return out.reshape(longest, comp), sums


def front_kernel(start_ref, compress_ref, x_ref, wq_ref, table_ref, c_ref, q_ref, wide):
    step = pl.program_id(0)

    longest = compress_ref.shape[0]

    @pl.when(step == 0)
    def _():
        wide[:longest, :] = compress_ref[...].astype(f32)
        wide[longest:, :] = jnp.zeros((TILE, wide.shape[1]), f32)

    rows = x_ref.shape[1]
    begin, shift = aligned(start_ref[step])
    window = wide[pl.ds(begin, rows + TILE), :]
    table = pltpu.roll(window, lax.rem(rows + TILE - shift, rows + TILE), 0)[:rows].astype(bf16)
    table_ref[0] = table
    x = x_ref[0]
    c_ref[0] = dot_tn(table, x).astype(bf16)
    q_ref[0] = (dot(x, wq_ref[...]) * SCALE).astype(bf16)


def front(starts, compress, x, wq):
    sets, rows, width = x.shape
    longest, comp = compress.shape
    grid_spec = pltpu.PrefetchScalarGridSpec(
        num_scalar_prefetch=1,
        grid=(sets,),
        in_specs=[whole(compress.shape), per_set((rows, width)), whole(wq.shape)],
        out_specs=[per_set((rows, comp)), per_set((comp, width)), per_set((rows, width))],
        scratch_shapes=[pltpu.VMEM((longest + TILE, comp), f32)],
    )
    return pl.pallas_call(
        front_kernel,
        grid_spec=grid_spec,
        out_shape=[
            jax.ShapeDtypeStruct((sets, rows, comp), bf16),
            jax.ShapeDtypeStruct((sets, comp, width), bf16),
            jax.ShapeDtypeStruct((sets, rows, width), bf16),
        ],
        compiler_params=params(),
        name="front",
    )(starts, compress, x, wq)


def head_blocks(pair, first_half):
    zero = jnp.zeros_like(pair)
    return jnp.concatenate([jnp.where(first_half, pair, zero), jnp.where(first_half, zero, pair)], axis=0)


def norm_forward(v):
    average = jnp.mean(v, axis=-1, keepdims=True)
    centered = v - average
    variance = jnp.mean(centered * centered, axis=-1, keepdims=True)
    inverse = lax.rsqrt(variance + EPS)
    return centered * inverse, inverse


def norm_backward(dz, z, inverse):
    return (dz - jnp.mean(dz, axis=-1, keepdims=True) - z * jnp.mean(dz * z, axis=-1, keepdims=True)) * inverse


def middle_kernel(
    c_ref, x_ref, q_ref, cot_ref, wk_ref, wv_ref, wo_ref, up_ref, down_ref, norms_ref,
    kc_ref, vc_ref, e_ref, mixed_ref, hidden_ref, act_ref, out_ref, gdown_ref, gup_ref,
    gfirst_ref, gatt_ref, go_ref, sums_ref,
    dgelu, z_first, rinv_ref,
):
    step = pl.program_id(0)
    rows, width = x_ref.shape[1:]
    comp = c_ref.shape[1]
    units = up_ref.shape[1]
    chunk = 768
    c = c_ref[0]
    kc_ref[0] = dot(c, wk_ref[...]).astype(bf16)
    vc_ref[0] = dot(c, wv_ref[...]).astype(bf16)
    half = lax.broadcasted_iota(jnp.int32, (comp, LANES), 1) < DH
    ones = head_blocks(jnp.ones((comp, LANES), bf16), half)
    for pair in range(width // LANES):
        lanes = pl.ds(pair * LANES, LANES)
        keys = head_blocks(kc_ref[0, :, lanes], half)
        values = jnp.concatenate([head_blocks(vc_ref[0, :, lanes], half), ones], axis=1)
        scores = dot_nt(q_ref[0, :, lanes], keys)
        parts = []
        for head in range(2):
            mine = scores[:, head * comp : (head + 1) * comp]
            top = jnp.max(mine, axis=-1, keepdims=True)
            parts.append(jnp.exp(mine - top).astype(bf16))
        e = jnp.concatenate(parts, axis=1)
        e_ref[0, :, pl.ds(pair * 2 * comp, 2 * comp)] = e
        sums = dot(e, values)
        rinv = 1.0 / sums[:, LANES:]
        rinv_ref[:, lanes] = rinv
        mixed_ref[0, :, lanes] = (sums[:, :LANES] * rinv).astype(bf16)
    gain1, bias1, gain2, bias2 = (norms_ref[i : i + 1, :] for i in range(4))
    z1, inv1 = norm_forward(x_ref[0].astype(f32) + dot(mixed_ref[0], wo_ref[...]))
    z_first[...] = z1
    hidden = z1 * gain1 + bias1
    hidden_low = hidden.astype(bf16)
    hidden_ref[0] = hidden_low
    gfirst_ref[0] = hidden
    for at in range(0, units, chunk):
        span = pl.ds(at, chunk)
        upward = dot(hidden_low, up_ref[:, span])
        cdf = 0.5 + 0.5 * lax.erf(upward * (0.5**0.5))
        density = jnp.exp(upward * upward * -0.5) * 0.3989422804014327
        act_ref[0, :, span] = (upward * cdf).astype(bf16)
        dgelu[:, span] = (cdf + upward * density).astype(bf16)
    z2, inv2 = norm_forward(gfirst_ref[0] + dot(act_ref[0], down_ref[...]))
    out_ref[0] = (z2 * gain2 + bias2).astype(bf16)
    dy = cot_ref[0].astype(f32)
    gsecond = norm_backward(dy * gain2, z2, inv2)
    gain2_part = jnp.sum(dy * z2, axis=0, keepdims=True)
    bias2_part = jnp.sum(dy, axis=0, keepdims=True)
    gdown = gsecond.astype(bf16)
    gdown_ref[0] = gdown
    gfirst_ref[0] = gsecond
    for at in range(0, units, chunk):
        span = pl.ds(at, chunk)
        gact = dot_nt(gdown, down_ref[span, :])
        gup_ref[0, :, span] = (gact * dgelu[:, span].astype(f32)).astype(bf16)
    ghidden = gfirst_ref[0] + dot_nt(gup_ref[0], up_ref[...])
    z1 = z_first[...]
    gfirst = norm_backward(ghidden * gain1, z1, inv1)
    gain1_part = jnp.sum(ghidden * z1, axis=0, keepdims=True)
    bias1_part = jnp.sum(ghidden, axis=0, keepdims=True)
    gfirst_ref[0] = gfirst
    gatt = gfirst.astype(bf16)
    gatt_ref[0] = gatt
    go_ref[0] = (dot_nt(gatt, wo_ref[...]) * rinv_ref[...]).astype(bf16)

    @pl.when(step == 0)
    def _():
        sums_ref[...] = jnp.zeros_like(sums_ref)

    for i, part in enumerate((gain1_part, bias1_part, gain2_part, bias2_part)):
        sums_ref[i : i + 1, :] += part


def middle(c, x, q, cot, wk, wv, wo, up, down, norms):
    sets, rows, width = x.shape
    comp = c.shape[1]
    units = up.shape[1]
    pairs = width // LANES
    outs = [
        ((comp, width), bf16),
        ((comp, width), bf16),
        ((rows, pairs * 2 * comp), bf16),
        ((rows, width), bf16),
        ((rows, width), bf16),
        ((rows, units), bf16),
        ((rows, width), bf16),
        ((rows, width), bf16),
        ((rows, units), bf16),
        ((rows, width), f32),
        ((rows, width), bf16),
        ((rows, width), bf16),
    ]
    return pl.pallas_call(
        middle_kernel,
        grid=(sets,),
        in_specs=[per_set((comp, width))] + [per_set((rows, width))] * 3
        + [whole(w.shape) for w in (wk, wv, wo, up, down, norms)],
        out_specs=[per_set(shape) for shape, _ in outs] + [whole((8, width))],
        out_shape=[jax.ShapeDtypeStruct((sets,) + shape, kind) for shape, kind in outs]
        + [jax.ShapeDtypeStruct((8, width), f32)],
        scratch_shapes=[
            pltpu.VMEM((rows, units), bf16),
            pltpu.VMEM((rows, width), f32),
            pltpu.VMEM((rows, width), f32),
        ],
        compiler_params=params(),
        name="middle",
    )(c, x, q, cot, wk, wv, wo, up, down, norms)


def attention_back_kernel(
    e_ref, go_ref, mixed_ref, q_ref, kc_ref, vc_ref, gfirst_ref, wq_ref, wk_ref, wv_ref,
    gq_ref, gk_ref, gv_ref, g_ref, gin_ref,
    gkt, gvt,
):
    width = q_ref.shape[2]
    comp = kc_ref.shape[1]
    half = lax.broadcasted_iota(jnp.int32, (comp, LANES), 1) < DH
    minus = head_blocks(jnp.full((comp, LANES), -1.0, bf16), half)
    for pair in range(width // LANES):
        lanes = pl.ds(pair * LANES, LANES)
        e = e_ref[0, :, pl.ds(pair * 2 * comp, 2 * comp)]
        keys = head_blocks(kc_ref[0, :, lanes], half)
        values = jnp.concatenate([head_blocks(vc_ref[0, :, lanes], half), minus], axis=1)
        go = go_ref[0, :, lanes]
        delta = (go.astype(f32) * mixed_ref[0, :, lanes].astype(f32)).astype(bf16)
        gp = dot_nt(jnp.concatenate([go, delta], axis=1), values)
        gs = (gp * e.astype(f32)).astype(bf16)
        gq_ref[0, :, lanes] = (dot(gs, keys) * SCALE).astype(bf16)
        for into, left, right in ((gkt, q_ref[0, :, lanes], gs), (gvt, go, e)):
            both = dot_tn(left, right)
            at = pair * LANES
            into[at : at + DH, :] = both[:DH, :comp].astype(bf16)
            into[at + DH : at + LANES, :] = both[DH:, comp:].astype(bf16)
    g_ref[0] = (dot(wk_ref[...], gkt[...]) + dot(wv_ref[...], gvt[...])).astype(bf16)
    gk_ref[0] = gkt[...].T
    gv_ref[0] = gvt[...].T
    gin_ref[0] = gfirst_ref[0] + dot_nt(gq_ref[0], wq_ref[...])


def attention_back(e, go, mixed, q, kc, vc, gfirst, wq, wk, wv):
    sets, rows, width = q.shape
    comp = kc.shape[1]
    outs = [
        ((rows, width), bf16),
        ((comp, width), bf16),
        ((comp, width), bf16),
        ((width, comp), bf16),
        ((rows, width), f32),
    ]
    tokens = per_set((rows, width))
    short = per_set((comp, width))
    return pl.pallas_call(
        attention_back_kernel,
        grid=(sets,),
        in_specs=[per_set(e.shape[1:])] + [tokens] * 3 + [short] * 2 + [tokens]
        + [whole(w.shape) for w in (wq, wk, wv)],
        out_specs=[per_set(shape) for shape, _ in outs],
        out_shape=[jax.ShapeDtypeStruct((sets,) + shape, kind) for shape, kind in outs],
        scratch_shapes=[pltpu.VMEM((width, comp), bf16)] * 2,
        compiler_params=params(),
        name="attention_back",
    )(e, go, mixed, q, kc, vc, gfirst, wq, wk, wv)


def feed_grads_kernel(hidden_ref, gup_ref, act_ref, gdown_ref, up_out, down_out):
    up_out[...] = dot_tn(hidden_ref[...], gup_ref[...]).astype(bf16)
    down_out[...] = dot_tn(act_ref[...], gdown_ref[...]).astype(bf16)


def feed_grads(hidden, gup, act, gdown):
    tokens, width = hidden.shape
    units = gup.shape[1]
    chunk = 512
    return pl.pallas_call(
        feed_grads_kernel,
        grid=(units // chunk,),
        in_specs=[
            whole((tokens, width)),
            pl.BlockSpec((tokens, chunk), lambda i: (0, i)),
            pl.BlockSpec((tokens, chunk), lambda i: (0, i)),
            whole((tokens, width)),
        ],
        out_specs=[
            pl.BlockSpec((width, chunk), lambda i: (0, i)),
            pl.BlockSpec((chunk, width), lambda i: (i, 0)),
        ],
        out_shape=[jax.ShapeDtypeStruct((width, units), bf16), jax.ShapeDtypeStruct((units, width), bf16)],
        compiler_params=params(),
        name="feed_grads",
    )(hidden, gup, act, gdown)


def square_grad_kernel(left_ref, right_ref, out_ref):
    out_ref[...] = dot_tn(left_ref[...], right_ref[...]).astype(bf16)


def square_grad(left, right):
    count, width = left.shape
    return pl.pallas_call(
        square_grad_kernel,
        grid=(1,),
        in_specs=[whole((count, width)), whole((count, width))],
        out_specs=whole((width, width)),
        out_shape=jax.ShapeDtypeStruct((width, width), bf16),
        compiler_params=params(),
        name="square_grad",
    )(left, right)


def last_kernel(start_ref, table_ref, x_ref, g_ref, gin_ref, out_ref, compress_ref, total):
    step = pl.program_id(0)

    @pl.when(step == 0)
    def _():
        total[...] = jnp.zeros_like(total)

    rows = x_ref.shape[1]
    g = g_ref[0]
    out_ref[0] = gin_ref[0] + dot_nt(table_ref[0], g)
    terms = dot(x_ref[0], g)
    begin, shift = aligned(start_ref[step])
    padded = jnp.concatenate([terms, jnp.zeros((TILE, terms.shape[1]), f32)], axis=0)
    total[pl.ds(begin, rows + TILE), :] += pltpu.roll(padded, shift, 0)

    @pl.when(step == pl.num_programs(0) - 1)
    def _():
        compress_ref[...] = total[: compress_ref.shape[0], :]


def last(starts, table, x, g, gin, longest):
    sets, rows, width = x.shape
    comp = table.shape[2]
    tokens = per_set((rows, width))
    grid_spec = pltpu.PrefetchScalarGridSpec(
        num_scalar_prefetch=1,
        grid=(sets,),
        in_specs=[per_set((rows, comp)), tokens, per_set((width, comp)), tokens],
        out_specs=[tokens, whole((longest, comp))],
        scratch_shapes=[pltpu.VMEM((longest + TILE, comp), f32)],
    )
    return pl.pallas_call(
        last_kernel,
        grid_spec=grid_spec,
        out_shape=[
            jax.ShapeDtypeStruct((sets, rows, width), f32),
            jax.ShapeDtypeStruct((longest, comp), f32),
        ],
        compiler_params=params(),
        name="last",
    )(starts, table, x, g, gin)


def sequence_sum(part, is_long, row_count, shortest):
    seq_count = lax.axis_size("seq")
    total = lax.psum(part, "seq")
    span = shortest // row_count
    if span > 1:
        groups = [list(range(i, i + span)) for i in range(0, seq_count, span)]
        part = lax.psum(part, "seq", axis_index_groups=groups)
    return jnp.where(is_long[:, None, None], total, part)


def table_start(set_kind, row_offset, block_index, row_count, shortest):
    position = block_index * row_count
    member = position // shortest
    chosen = jnp.sum(jnp.where(jnp.arange(4)[None, :] == member, row_offset, 0), axis=1)
    return jnp.where(set_kind > 0, position, chosen + position % shortest)


def local(
    inputs, cotangent, set_kind, row_offset, query_w, key_w, value_w, output_w, up_w, down_w, compress,
    first_gain, first_bias, second_gain, second_bias,
):
    sets, rows, width = inputs.shape
    longest, comp = compress.shape
    shortest = longest // 4
    ranked = lax.axis_index("seq")
    tokens = sets * rows
    is_long = set_kind > 0
    starts = table_start(set_kind, row_offset, ranked, rows, shortest).astype(jnp.int32)
    norms = jnp.concatenate(
        [jnp.stack([first_gain, first_bias, second_gain, second_bias]), jnp.zeros((4, width), f32)], axis=0
    )
    table, part, queries = front(starts, compress, inputs, query_w)
    linked = lax.axis_size("batch") == 8 and lax.axis_size("seq") == 4 and rows == shortest
    if linked:
        summed = line_sum(part, set_kind, 0)
    else:
        summed = sequence_sum(part, is_long, rows, shortest)
    (kc, vc, e, mixed, hidden, act, layer_out, gdown, gup, gfirst, gatt, go, norm_sums) = middle(
        summed, inputs, queries, cotangent, key_w, value_w, output_w, up_w, down_w, norms
    )
    flat = lambda v: v.reshape(-1, v.shape[-1])
    up_part, down_part = feed_grads(flat(hidden), flat(gup), flat(act), flat(gdown))
    output_part = square_grad(flat(mixed), flat(gatt))
    gq, gk, gv, g_part, gin = attention_back(
        e, go, mixed, queries, kc, vc, gfirst, query_w, key_w, value_w
    )
    if linked:
        g = line_sum(g_part, set_kind, 1)
    else:
        g = sequence_sum(g_part, is_long, rows, shortest)
    query_part = square_grad(flat(inputs), flat(gq))
    key_part = square_grad(flat(summed), flat(gk))
    value_part = square_grad(flat(summed), flat(gv))
    input_grad, compress_part = last(starts, table, inputs, g, gin, longest)

    def scattered(v):
        v = lax.psum_scatter(v, "seq", scatter_dimension=1, tiled=True)
        return lax.psum_scatter(v, "batch", scatter_dimension=0, tiled=True).astype(f32)

    parts = (query_part, key_part, value_part, output_part, up_part, down_part)
    if linked:
        weights = tuple(scatter(*parts))
        compress_grad, norm_grads = total_sum(compress_part, norm_sums)
    else:
        weights = tuple(scattered(v) for v in parts)
        compress_grad, norm_grads = lax.psum((compress_part, norm_sums), ("batch", "seq"))
    return (layer_out, input_grad) + weights + (compress_grad,) + tuple(norm_grads[i] for i in range(4))


def solution(mesh):
    tokens = P("batch", "seq", None)
    in_specs = (tokens, tokens, P("batch"), P("batch", None)) + (P(),) * 11
    out_specs = (tokens, tokens) + (P("batch", "seq"),) * 6 + (P(),) * 5
    return jax.shard_map(local, mesh=mesh, in_specs=in_specs, out_specs=out_specs, check_vma=False)
```

time: 1410 us -> 441 us (0.31)
  waiting for transfers between devices: 779 us -> 0 us
  Pallas kernels: 0 us -> 416 us
  matrix products: 311 us -> 0 us
  local copies, waits for them, and re-layouts: 129 us -> 17.7 us
  other arithmetic: 107 us -> 1.97 us
  blocking collectives: 41.9 us -> 0 us
  between operations: 24.6 us -> 1.16 us
    pallas_call x0 -> x13, Pallas kernels: none -> 416 us  [the longest x1 110 us: scatter(): pl.pallas_call(functools.partial(scatter_kernel, line), in_specs=[vmem] *...]
    ppermute x6 -> x0, waiting for transfers between devices: 408 us -> none  [shifted(): return lax.ppermute(block, axis, route)]
    dot_general x21 -> x0, matrix products: 311 us -> none  [the longest x4 68.5 us: contract_cols(): lax.dot_general(left_in, right_in, (((1,), (1,)), ((), ())), preferred_el...]
    reduce_scatter x7 -> x0, waiting for transfers between devices: 279 us -> none  [the longest x1 85.4 us: local(): lax.psum_scatter(up_part.astype(jnp.bfloat16), 'seq', scatter_dimension=1...]
    unnamed x18 -> x0, waiting for transfers between devices: 91.7 us -> none
    add x10 -> x0, other arithmetic: 43.4 us -> none  [the longest x3 26 us: cycle_back(): return (travel, running + jnp.where(joined[:, None, None], travel, 0.0))]
    psum x1 -> x0, blocking collectives: 41.9 us -> none  [local(): lax.psum((compress_part, first_gain_part, first_bias_part, second_gain_pa...]
    convert_element_type x4 -> x0, other arithmetic: 27.1 us -> none  [the longest x1 21.6 us: local(): grad_scores = (probs * (grad_probs - row_delta)).astype(jnp.bfloat16)]
  transfers between devices with their start and end apart: 19 -> 0, of which waited for: 15 -> 0; matrix products, arithmetic and copies ran while one was open for 7% -> 0% of each run, Pallas kernels for 0% -> 0%
where the time goes in v1:
time: 441 us; the launch traced here: 437 us
  Pallas kernels  416 us (94%)
  local copies, waits for them, and re-layouts  17.7 us (4%)
    pallas_call x1, Pallas kernels, scatter(): pl.pallas_call(functools.partial(scatter_kernel, line), in_specs=[vmem] *...  110 us
    pallas_call x2, Pallas kernels, line_sum(): pl.pallas_call(functools.partial(line_sum_kernel, line), in_specs=[vmem,...  98.2 us
    pallas_call x1, Pallas kernels, middle(): pl.pallas_call(middle_kernel, grid=(sets,), in_specs=[per_set((comp, widt...  83.9 us
    pallas_call x1, Pallas kernels, total_sum(): pl.pallas_call(functools.partial(total_kernel, line), in_specs=[vmem] * 2...  34.2 us
    pallas_call x1, Pallas kernels, feed_grads(): pl.pallas_call(feed_grads_kernel, grid=(units // chunk,), in_specs=[whole...  25.9 us
    pallas_call x1, Pallas kernels, attention_back(): pl.pallas_call(attention_back_kernel, grid=(sets,), in_specs=[per_set(e.s...  24 us
    pallas_call x4, Pallas kernels, square_grad(): pl.pallas_call(square_grad_kernel, grid=(1,), in_specs=[whole((count, wid...  21.7 us
    unnamed x7, local copies, waits for them, and re-layouts  12.8 us

profile of v1, /device:TPU:0, one launch (start us, length us, event | category | flops | bytes accessed | tf_op | source)
XLA Modules:
  0.0 437.3 jit_solution(5305335939131069830)
XLA Ops:
  0.7 0.8 select_reduce_fusion
  1.5 1.2 compare_select_fusion.start_ref
  2.6 0.7 stack.12
  3.3 0.7 stack.13
  4.0 0.7 stack.14
  4.7 0.7 stack.15
  5.4 0.6 concatenate.3.norms_ref
  6.0 8.8 %front.1 = (bf16[4,512,256]{2,1,0:T(8,128)(2,1)}, bf16[4,256,768]{2,1,0:T(8,128)(2,1)}, bf16[4,512,768]{2,1,0:T(8,128)(2,1)}) custom-call(s32[4]{0:T(128)} %compare_select_fusion.start_ref, bf16[2048,256]{1,0:T(8,128)(2,1)} %compress_ref.1, bf16[4,512,768]{2,1,0:T(8,128)(2,1)} %x_ref.5, bf16[768,768]{1,0:T(8,128)(2,1)} %wq_ref.3), custom_call_target="tpu_custom_call" | custom-call | tf_op jit(solution)/shard_map/front/pallas_call | solution.py:435
  14.8 50.4 %line_sum.2 = bf16[16,64,768]{2,1,0:T(8,128)(2,1)} custom-call(bf16[16,64,768]{2,1,0:T(8,128)(2,1)} %bitcast.46, s32[4]{0:T(128)} %long_ref.3), custom_call_target="tpu_custom_call" | custom-call | tf_op jit(solution)/shard_map/line_sum/pallas_call | solution.py:161
  65.3 83.9 %middle.1 = (bf16[4,256,768]{2,1,0:T(8,128)(2,1)}, bf16[4,256,768]{2,1,0:T(8,128)(2,1)}, bf16[4,512,3072]{2,1,0:T(8,128)(2,1)}, bf16[4,512,768]{2,1,0:T(8,128)(2...) custom-call(bf16[4,256,768]{2,1,0:T(8,128)(2,1)} %bitcast.24, ...), custom_call_target="tpu_custom_call" | custom-call | tf_op jit(solution)/shard_map/middle/pallas_call | solution.py:561
  149.2 6.5 %square_grad.7 = bf16[768,768]{1,0:T(8,128)(2,1)} custom-call(bf16[2048,768]{1,0:T(8,128)(2,1)} %bitcast.27, bf16[2048,768]{1,0:T(8,128)(2,1)} %bitcast.38), custom_call_target="tpu_custom_call" | custom-call | tf_op jit(solution)/shard_map/square_grad/pallas_call | solution.py:668
  155.7 25.9 %feed_grads.1 = (bf16[768,3072]{1,0:T(8,128)(2,1)}, bf16[3072,768]{1,0:T(8,128)(2,1)}) custom-call(bf16[2048,768]{1,0:T(8,128)(2,1)} %bitcast.39, bf16[2048,3072]{1,0:T(8,128)(2,1)} %bitcast.29, bf16[2048,3072]{1,0:T(8,128)(2,1)} %bitcast.28, bf16[2048,768]{1,0:T(8,128)(2,1)} %bitcast.40), custom_call_target="tpu_custom_call" | custom-call | tf_op jit(solution)/shard_map/feed_grads/pallas_call | solution.py:643
  181.7 24.0 %attention_back.1 = (bf16[4,512,768]{2,1,0:T(8,128)(2,1)}, bf16[4,256,768]{2,1,0:T(8,128)(2,1)}, bf16[4,256,768]{2,1,0:T(8,128)(2,1)}, bf16[4,768,256]{2,1,0:T(8,128)(2,1)}, f32[4,512,768]{2,1,0:T(8,128)}) custom-call(bf16[4,512,3072]{2,1,0:T(8,128)(2,1)} %get-tuple-element.50.e_ref, bf16[4,512,768]{2,1,0:T(8,128)(2,1)} %get-tuple-element.51.go_ref, ...), custom_call_target="tpu_custom_call" | custom-call | tf_op jit(solution)/shard_map/attention_back/pallas_call | solution.py:621
  205.7 47.8 %line_sum.3 = bf16[16,192,256]{2,1,0:T(8,128)(2,1)} custom-call(bf16[16,192,256]{2,1,0:T(8,128)(2,1)} %bitcast.45, s32[4]{0:T(128)} %long_ref.3), custom_call_target="tpu_custom_call" | custom-call | tf_op jit(solution)/shard_map/line_sum/pallas_call | solution.py:161
  253.5 10.0 %last.1 = (f32[4,512,768]{2,1,0:T(8,128)}, f32[2048,256]{1,0:T(8,128)}) custom-call(s32[4]{0:T(128)} %compare_select_fusion.start_ref, bf16[4,512,256]{2,1,0:T(8,128)(2,1)} %get-tuple-element.49.table_ref, bf16[4,512,768]{2,1,0:T(8,128)(2,1)} %x_ref.5, bf16[4,768,256]{2,1,0:T(8,128)(2,1)} %bitcast.30, f32[4,512,768]{2,1,0:T(8,128)} %get-tuple-element.57.gin_ref), custom_call_target="tpu_custom_call" | custom-call | tf_op jit(solution)/shard_map/last/pallas_call | solution.py:710
  263.5 34.2 %total_sum.1 = (f32[2,4,4,64,256]{4,3,2,1,0:T(8,128)}, f32[8,768]{1,0:T(8,128)}) custom-call(f32[2,4,4,64,256]{4,3,2,1,0:T(8,128)} %bitcast.42, f32[8,768]{1,0:T(8,128)} %get-tuple-element.76.norms_ref), custom_call_target="tpu_custom_call" | custom-call | tf_op jit(solution)/shard_map/total_sum/pallas_call | solution.py:383
  297.8 1.5 slice_reduce_fusion
  299.3 6.5 %square_grad.4 = bf16[768,768]{1,0:T(8,128)(2,1)} custom-call(bf16[2048,768]{1,0:T(8,128)(2,1)} %bitcast.23, bf16[2048,768]{1,0:T(8,128)(2,1)} %bitcast.37), custom_call_target="tpu_custom_call" | custom-call | tf_op jit(solution)/shard_map/square_grad/pallas_call | solution.py:668
  305.8 4.3 square_grad.5
  310.1 4.4 %square_grad.6 = bf16[768,768]{1,0:T(8,128)(2,1)} custom-call(bf16[1024,768]{1,0:T(8,128)(2,1)} %bitcast.26, bf16[1024,768]{1,0:T(8,128)(2,1)} %bitcast.43), custom_call_target="tpu_custom_call" | custom-call | tf_op jit(solution)/shard_map/square_grad/pallas_call | solution.py:668
  314.5 109.6 %scatter.1 = (f32[96,192]{1,0:T(8,128)}, f32[96,192]{1,0:T(8,128)}, f32[96,192]{1,0:T(8,128)}, f32[96,192]{1,0:T(8,128)}, f32[96,768]{1,0:T(8,128)}, /*index=5*/f32[384,192]{1,0:T(8,128)}) custom-call(bf16[2,2,2,96,768]{4,3,2,1,0:T(8,128)(2,1)} %bitcast.32, bf16[2,2,2,96,768]{4,3,2,1,0:T(8,128)(2,1)} %bitcast.35, bf16[2,2,2,96,768]{4,3,2,1,0:T(8,128)(2,1)} %bitcast.36, ...), custom_call_target="tpu_custom_call" | custom-call | tf_op jit(solution)/shard_map/scatter/pallas_call | solution.py:306
  424.1 1.9 copy.28
  425.9 1.5 copy.35
  427.5 1.5 copy.36
  429.0 1.5 copy.37
  430.6 1.5 copy.38
  432.1 1.7 copy.39
  433.8 3.0 copy.40
  (2 shorter events, 0.0 us)
